TPU v7x, 32 devices: a whole 2x2x4 slice. The times are simulated.
32 devices in a mesh: ctx: 8 (over y, x, core), vocab: 4 (over z).
Axes of the slice: x: 2, y: 2, z: 4, core: 2. Of those that a mesh axis runs over, the one named last changes fastest.
Arguments:
- query_rows: bfloat16 [2048, 4096], P('ctx', 'vocab'), may hold values from -12 to 12
- key_rows: bfloat16 [2048, 2048], P('ctx', 'vocab'), may hold values from -6 to 6
- value_rows: bfloat16 [2048, 2048], P('ctx', 'vocab'), may hold values from -6 to 6
- residual: bfloat16 [2048, 4608], P('ctx', 'vocab'), may hold values from -6 to 6
- out_weight: bfloat16 [4096, 4608], P('vocab'), may hold values from -0.09375 to 0.09375
- post_gain: float32 [4608], P('vocab'), may hold values from 0.1 to 1.9
- final_gain: float32 [4608], P('vocab'), may hold values from 0.1 to 1.9
- embedding: bfloat16 [32768, 4608], P(('ctx', 'vocab')), may hold values from -0.25 to 0.25
- targets: int32 [64], P('ctx'), may hold values from 0 to 32767
- loss_mask: int32 [64], P('ctx'), may hold values 0 or 1
- pick_pos: int32 [64], P('ctx'), may hold values from 0 to 255, as said below
Outputs:
- final_hidden: bfloat16 [2048, 4608], P('ctx', 'vocab')
- mean_loss: float32 [], replicated
- grad_normed: float32 [64, 4608], P('ctx', 'vocab')
Inputs may be any that keep to these rules, and one draw needn't show every extreme that they name: `pick_pos`: entry k is a position inside the block of 256 tokens held by index k // 8 of ctx; entries may repeat.
All inputs are finite; a program needn't handle non-finite values. No bound on the sum of `loss_mask` on one device may be relied on, other than what follows from the above.
Results may differ from a plain program's by a relative error of at most 0.0049.
Values may be sent and summed in bfloat16 or wider, within the bound.
A program may use at most 256 MiB of HBM per device.

v0:
```python
import jax
import jax.numpy as jnp
from jax import lax
from jax.sharding import PartitionSpec as P

D = 4608
HEADS = 32
KV_HEADS = 16
HEAD_DIM = 128
WINDOW = 4096


attn_cap = 50.0
logit_cap = 30.0
query_scalar = 144.0
epsilon = 1e-06


def attend(key_value, query_grp, query_pos):
    piece_len = key_value.shape[1]
    kv_local = query_grp.shape[1]
    key_piece = key_value[0].reshape(piece_len, kv_local, HEAD_DIM)
    value_piece = key_value[1].reshape(piece_len, kv_local, HEAD_DIM)
    raw_scores = jnp.einsum(
        "tgcd,sgd->gcts", query_grp, key_piece, preferred_element_type=jnp.float32
    )
    capped = attn_cap * jnp.tanh(raw_scores * query_scalar ** (-0.5) / attn_cap)
    key_pos = jnp.arange(piece_len, dtype=jnp.int32)
    distance = query_pos[:, None] - key_pos[None, :]
    allowed = (distance >= 0) & (distance < WINDOW) & (key_pos[None, :] >= 0)
    weights = jnp.where(allowed, jnp.exp(capped), 0.0)
    acc_weights = jnp.sum(weights, axis=-1)
    acc_values = jnp.einsum(
        "gcts,sgd->gctd",
        weights.astype(jnp.bfloat16),
        value_piece,
        preferred_element_type=jnp.float32,
    )
    return (acc_values, acc_weights)


def shards(
    query_rows,
    key_rows,
    value_rows,
    residual,
    out_weight,
    post_gain,
    final_gain,
    embedding,
    targets,
    loss_mask,
    pick_pos,
):
    local_len = query_rows.shape[0]
    group_size = HEADS // KV_HEADS
    kv_local = key_rows.shape[1] // HEAD_DIM
    ctx_index = lax.axis_index("ctx")
    query_grp = query_rows.reshape(local_len, kv_local, group_size, HEAD_DIM)
    query_pos = ctx_index * local_len + jnp.arange(local_len, dtype=jnp.int32)
    key_value = jnp.stack((key_rows, value_rows))
    initial = (
        jnp.zeros((kv_local, group_size, local_len, HEAD_DIM), jnp.float32),
        jnp.zeros((kv_local, group_size, local_len), jnp.float32),
    )
    first_query = ctx_index * local_len
    last_query = first_query + local_len - 1
    piece = lax.all_gather(key_value, "ctx", axis=1, tiled=True)
    offset = jnp.int32(0)
    piece_len = piece.shape[1]
    needed = (offset <= last_query) & (offset + piece_len - 1 > first_query - WINDOW)

    def work(state_now):
        return attend(piece, query_grp, query_pos)

    def skip(state_now):
        return state_now

    acc_values, acc_weights = lax.cond(needed, work, skip, initial)
    attended = acc_values / acc_weights[..., None]
    attended = jnp.transpose(attended, (2, 0, 1, 3)).reshape(
        local_len, kv_local * group_size * HEAD_DIM
    )
    attended = attended.astype(jnp.bfloat16)
    partial_proj = jnp.dot(attended, out_weight, preferred_element_type=jnp.float32)
    own_cols = lax.psum_scatter(partial_proj, "vocab", scatter_dimension=1, tiled=True)
    square_sum = lax.psum(jnp.sum(own_cols * own_cols, axis=1, keepdims=True), "vocab")
    inv_rms = lax.rsqrt(square_sum / D + epsilon)
    final_hidden = (residual.astype(jnp.float32) + own_cols * inv_rms * post_gain).astype(
        jnp.bfloat16
    )
    picked = jnp.take(final_hidden, pick_pos, axis=0).astype(jnp.float32)
    picked_sum = lax.psum(jnp.sum(picked * picked, axis=1, keepdims=True), "vocab")
    normed = (picked * lax.rsqrt(picked_sum / D + epsilon) * final_gain).astype(jnp.bfloat16)
    normed_full = lax.all_gather(normed, "vocab", axis=1, tiled=True)
    all_targets, all_mask = (
        lax.all_gather(targets, "ctx", axis=0, tiled=True),
        lax.all_gather(loss_mask, "ctx", axis=0, tiled=True),
    )
    raw_logits = jnp.einsum(
        "td,vd->tv",
        lax.all_gather(normed_full, "ctx", axis=0, tiled=True),
        embedding,
        preferred_element_type=jnp.float32,
    )
    logits = logit_cap * jnp.tanh(raw_logits / logit_cap)
    vocab_local = embedding.shape[0]
    vocab_base = (ctx_index * lax.axis_size("vocab") + lax.axis_index("vocab")) * vocab_local
    onehot = (vocab_base + jnp.arange(vocab_local, dtype=jnp.int32))[None, :] == all_targets[
        :, None
    ]
    exp_logits = jnp.exp(logits)
    local_total = jnp.sum(exp_logits, axis=1)
    local_target = jnp.sum(jnp.where(onehot, logits, 0.0), axis=1)
    totals, target_logit = lax.psum((local_total, local_target), ("ctx", "vocab"))
    mask_float = all_mask.astype(jnp.float32)
    mean_loss = jnp.sum(mask_float * (jnp.log(totals) - target_logit)) / all_targets.shape[0]
    dlogits = mask_float[:, None] * (exp_logits / totals[:, None] - onehot.astype(jnp.float32))
    dlogits = (dlogits * (1.0 - (logits / logit_cap) ** 2)).astype(jnp.bfloat16)
    partial_grad = jnp.dot(dlogits, embedding, preferred_element_type=jnp.float32)
    by_features = lax.psum_scatter(partial_grad, "vocab", scatter_dimension=1, tiled=True)
    grad_normed = lax.psum_scatter(by_features, "ctx", scatter_dimension=0, tiled=True)
    return (final_hidden, mean_loss, grad_normed)


def solution(mesh):
    in_specs = (
        P("ctx", "vocab"),
        P("ctx", "vocab"),
        P("ctx", "vocab"),
        P("ctx", "vocab"),
        P("vocab", None),
        P("vocab"),
        P("vocab"),
        P(("ctx", "vocab"), None),
        P("ctx"),
        P("ctx"),
        P("ctx"),
    )
    out_specs = (P("ctx", "vocab"), P(), P("ctx", "vocab"))
    return jax.shard_map(shards, mesh=mesh, in_specs=in_specs, out_specs=out_specs, check_vma=False)
```

profile of v0, /device:TPU:0, one launch (start us, length us, event | category | flops | bytes accessed | tf_op | source)
XLA Modules:
  0.0 355.1 jit_solution(8098362487231117743)
XLA Ops:
  7.2 1.1 copy.28
  8.3 1.1 copy.29
  9.4 0.8 pad_maximum_fusion
  10.3 40.3 %all-gather.2.cloned.1.call-done = bf16[2,2048,512]{1,2,0:T(8,128)(2,1)} async-done(((bf16[2,256,512]{1,2,0:T(8,128)(2,1)}), bf16[2,2048,512]{1,2,0:T(8,128)(2,1)}) %all-gather.2.cloned.1.call-update) | async-done | bytes 4194320 | tf_op jit(solution)/shard_map/all_gather | solution.py:68
  50.6 18.9 %conditional.1 = (f32[4,2,256]{2,1,0:T(2,128)S(1)}, f32[4,2,256,128]{2,3,1,0:T(8,128)S(1)}) conditional(s32[]{:T(128)} %convert_element_type.37, () %tuple.16, (s32[]{:T(128)}, s32[256]{0:T(256)S(1)}, bf16[2,2048,512]{1,2,0:T(8,128)(2,1)}, bf16[256,1024]{1,0:T(8,128)(2,1)}) %tuple.17), branch_computations={%region_0.0_spmd, %region_1.3_spmd} | conditional | flops 2183133440 | bytes 54537292 | solution.py:79
  50.6 4.1 %fusion.32 = (bf16[1,2048,512]{1,2,0:T(8,128)(2,1)S(1)}, bf16[1,2048,512]{1,2,0:T(8,128)(2,1)}) fusion(bf16[2,2048,512]{1,2,0:T(8,128)(2,1)} %get-tuple-element.13), kind=kLoop, calls=%fused_computation.53 | loop fusion | bytes 8388608 | tf_op jit(solution)/shard_map/cond/branch_1_fun/slice | solution.py:23
  55.3 1.2 reshape.27
  56.4 6.8 %fusion = (f32[4,2,256]{2,1,0:T(2,128)S(1)}, f32[4,2048,256,2]{2,1,3,0:T(8,128)S(1)}) fusion(pred[256,2048]{0,1:T(8,128)(4,1)S(1)} %fusion.7, bf16[2048,4,128,1]{0,2,3,1:T(8,128)(2,1)} %bitcast.38, bf16[256,4,2,128]{3,2,1,0:T(2,128)(2,1)} %reshape.27), kind=kOutput, calls=%fused_computation.2 | convolution fusion | flops 1090516992 | bytes 19931136 | tf_op jit(solution)/shard_map/cond/branch_1_fun/tgcd,sgd->gcts/dot_general | solution.py:24
  63.3 6.2 %fusion.2 = f32[4,2,256,128]{2,3,1,0:T(8,128)S(1)} fusion(bf16[2048,4,128,1]{0,2,3,1:T(8,128)(2,1)S(1)} %bitcast.37, f32[4,2048,256,2]{2,1,3,0:T(8,128)S(1)} %get-tuple-element.34, pred[256,2048]{0,1:T(8,128)(4,1)} %copy-done.3), kind=kOutput, calls=%fused_computation.4 | convolution fusion | flops 1090519040 | bytes 20447232 | tf_op jit(solution)/shard_map/cond | solution.py:79
  69.7 8.0 %fusion.34 = f32[256,4608]{1,0:T(8,128)} fusion(bf16[256,1024]{0,1:T(8,128)(2,1)S(1)} %bitcast.36, bf16[1024,4608]{1,0:T(8,128)(2,1)} %param.17), kind=kOutput, calls=%fused_computation.55 | convolution fusion | flops 2415919104 | bytes 14680064 | tf_op jit(solution)/shard_map/dot_general | solution.py:85
  79.5 7.0 %all-reduce.3 = (s32[64]{0:T(128)S(1)}, s32[64]{0:T(128)S(1)}) all-reduce(s32[64]{0:T(128)S(1)} %dynamic-update-slice.1, s32[64]{0:T(128)S(1)} %dynamic-update-slice), channel_id=1, replica_groups=mesh['ctx'=8,'vocab'=4] {'ctx'}, use_global_device_ids=true, to_apply=%add.1 | all-reduce | flops 128 | bytes 1024
  86.6 76.5 %reduce-scatter.3.cloned.1.call-done = f32[256,1152]{1,0:T(8,128)} async-done(((f32[256,4608]{1,0:T(8,128)}), f32[256,1152]{1,0:T(8,128)}) %reduce-scatter.3.cloned.1.call-update) | async-done | bytes 1179664 | tf_op jit(solution)/shard_map/reduce_scatter | solution.py:86
  163.2 1.4 multiply_reduce_fusion
  164.6 10.9 %psum.28 = f32[256,1]{0,1:T(1,128)S(1)} all-reduce(f32[256,1]{0,1:T(1,128)S(1)} %bitcast.42), channel_id=1, replica_groups=mesh['ctx'=8,'vocab'=4] {'vocab'}, use_global_device_ids=true, to_apply=%region_5.6 | all-reduce | flops 256 | bytes 2048 | tf_op jit(solution)/shard_map/psum | solution.py:87
  175.5 1.5 add_convert_fusion
  177.8 8.4 %psum.29 = f32[8,1]{0,1:T(1,128)S(1)} all-reduce(f32[8,1]{0,1:T(1,128)S(1)} %bitcast.43), channel_id=1, replica_groups=mesh['ctx'=8,'vocab'=4] {'vocab'}, use_global_device_ids=true, to_apply=%region_7.8 | all-reduce | flops 8 | bytes 64 | tf_op jit(solution)/shard_map/psum | solution.py:93
  186.3 13.2 %all_gather.17 = bf16[8,4608]{1,0:T(8,128)(2,1)S(1)} all-gather(bf16[8,1152]{1,0:T(8,128)(2,1)S(1)} %fusion.29), channel_id=1, replica_groups=mesh['ctx'=8,'vocab'=4] {'vocab'}, dimensions={1}, use_global_device_ids=true | all-gather | bytes 92160 | tf_op jit(solution)/shard_map/all_gather | solution.py:95
  199.4 10.4 %all_gather.18 = bf16[64,4608]{1,0:T(8,128)(2,1)S(1)} all-gather(bf16[8,4608]{1,0:T(8,128)(2,1)S(1)} %all_gather.17), channel_id=1, replica_groups=mesh['ctx'=8,'vocab'=4] {'ctx'}, dimensions={0}, use_global_device_ids=true | all-gather | bytes 663552 | tf_op jit(solution)/shard_map/all_gather | solution.py:102
  209.8 6.8 %exponential_reduce_fusion = (f32[64]{0:T(128)S(1)}, f32[64]{0:T(128)S(1)}, f32[64,1024]{1,0:T(8,128)S(1)}) fusion(s32[64]{0:T(128)S(1)} %get-tuple-element.27, s32[1024]{0:T(1024)S(1)} %iota_add_fusion, bf16[64,4608]{1,0:T(8,128)(2,1)S(1)} %all_gather.18, bf16[1024,4608]{1,0:T(8,128)(2,1)} %param.20), kind=kOutput, calls=%fused_computation.29 | convolution fusion | flops 604372864 | bytes 10294016 | tf_op jit(solution)/shard_map/td,vd->tv/dot_general | solution.py:100
  216.6 38.0 %all-reduce.4 = (f32[64]{0:T(128)S(1)}, f32[64]{0:T(128)S(1)}) all-reduce(f32[64]{0:T(128)S(1)} %get-tuple-element.26, f32[64]{0:T(128)S(1)} %get-tuple-element.25), channel_id=1, replica_groups=mesh['ctx'=8,'vocab'=4] {'ctx','vocab'}, use_global_device_ids=true, to_apply=%region_11.12 | all-reduce | flops 128 | bytes 1024 | tf_op jit(solution)/shard_map/psum | solution.py:115
  254.6 6.5 %fusion.19 = f32[64,4608]{1,0:T(8,128)} fusion(bf16[1024,4608]{1,0:T(8,128)(2,1)} %param.20, f32[64,1024]{1,0:T(8,128)S(1)} %get-tuple-element.37, f32[64]{0:T(128)S(1)} %get-tuple-element.30, f32[64]{0:T(128)S(1)} %convert_element_type.42, s32[1024]{0:T(1024)S(1)} %iota_add_fusion, s32[64]{0:T(128)S(1)} %get-tuple-element.27), kind=kOutput, calls=%fused_computation.30 | convolution fusion | flops 604635136 | bytes 10883840 | tf_op jit(solution)/shard_map/dot_general | solution.py:120
  261.2 30.1 %reduce-scatter.5.cloned.1.call-done = f32[64,1152]{1,0:T(8,128)} async-done(((f32[64,4608]{1,0:T(8,128)}), f32[64,1152]{1,0:T(8,128)}) %reduce-scatter.5.cloned.1.call-update) | async-done | bytes 294928 | tf_op jit(solution)/shard_map/reduce_scatter | solution.py:121
  293.2 52.8 %all-reduce.7.cloned.1.call-done = f32[64,1152]{1,0:T(8,128)} async-done(((f32[64,1152]{1,0:T(8,128)}), f32[64,1152]{1,0:T(8,128)}) %all-reduce.7.cloned.1.call-update) | async-done | bytes 294928
  346.0 1.4 constant_dynamic-slice_fusion
  (48 shorter events, 3.5 us)
Async XLA Ops:
  7.2 43.5 %all-gather.2.cloned.1.call-start = ((), (), s32[]{:S(2)}) async-start(), calls=%async_computation.2 | async-start | bytes 4718592 | tf_op jit(solution)/shard_map/all_gather | solution.py:68
  10.3 152.9 %reduce-scatter.3.cloned.1.call-start = ((), (), s32[]{:S(2)}) async-start(), calls=%async_computation.3 | async-start | bytes 5898240 | tf_op jit(solution)/shard_map/reduce_scatter | solution.py:86
  50.6 4.6 %copy-start.2 = (bf16[256,1024]{1,0:T(8,128)(2,1)S(1)}, bf16[256,1024]{1,0:T(8,128)(2,1)}, u32[]{:S(2)}) copy-start(bf16[256,1024]{1,0:T(8,128)(2,1)} %get-tuple-element.23) | copy-start | bytes 1572868 | tf_op jit(solution)/shard_map/cond
  55.2 8.0 %copy-start.3 = (pred[256,2048]{0,1:T(8,128)(4,1)}, pred[256,2048]{0,1:T(8,128)(4,1)S(1)}, u32[]{:S(2)}) copy-start(pred[256,2048]{0,1:T(8,128)(4,1)S(1)} %fusion.7) | copy-start | bytes 1572868 | tf_op jit(solution)/shard_map/cond
  69.6 8.2 %copy-start.6 = (u32[32]{0:T(128)S(1)}, u32[32]{0:T(128)}, u32[]{:S(2)}) copy-start(u32[32]{0:T(128)} %constant.79) | copy-start | bytes 388
  69.6 9.4 %copy-start.7 = (s32[8]{0:T(128)S(1)}, s32[8]{0:T(128)}, u32[]{:S(2)}) copy-start(s32[8]{0:T(128)} %param.22) | copy-start | bytes 100
  69.6 9.7 %copy-start.8 = (s32[8]{0:T(128)S(1)}, s32[8]{0:T(128)}, u32[]{:S(2)}) copy-start(s32[8]{0:T(128)} %param.21) | copy-start | bytes 100
  69.6 16.9 %copy-start.9 = (s32[8]{0:T(128)S(1)}, s32[8]{0:T(128)}, u32[]{:S(2)}) copy-start(s32[8]{0:T(128)} %param.23) | copy-start | bytes 100
  69.6 105.9 %copy-start.1 = (bf16[256,1152]{1,0:T(8,128)(2,1)S(1)}, bf16[256,1152]{1,0:T(8,128)(2,1)}, u32[]{:S(2)}) copy-start(bf16[256,1152]{1,0:T(8,128)(2,1)} %param.16) | copy-start | bytes 1769476
  69.7 105.9 %copy-start.4 = (f32[1152]{0:T(1024)S(1)}, f32[1152]{0:T(1024)}, u32[]{:S(2)}) copy-start(f32[1152]{0:T(1024)} %param.18) | copy-start | bytes 13828
  69.7 116.5 %copy-start.5 = (f32[1152]{0:T(1024)S(1)}, f32[1152]{0:T(1024)}, u32[]{:S(2)}) copy-start(f32[1152]{0:T(1024)} %param.19) | copy-start | bytes 13828
  77.7 213.5 %reduce-scatter.5.cloned.1.call-start = ((), (), s32[]{:S(2)}) async-start(), calls=%async_computation.4 | async-start | bytes 1474560 | tf_op jit(solution)/shard_map/reduce_scatter | solution.py:121
  177.1 84.1 %copy-start = (bf16[256,1152]{1,0:T(8,128)(2,1)}, bf16[256,1152]{1,0:T(8,128)(2,1)S(1)}, u32[]{:S(2)}) copy-start(bf16[256,1152]{1,0:T(8,128)(2,1)S(1)} %add_convert_fusion) | copy-start | bytes 1769476
  261.1 84.9 %all-reduce.7.cloned.1.call-start = ((), (), s32[]{:S(2)}) async-start(), calls=%async_computation.5 | async-start | bytes 589824
Sparse Core Ops, SparseCore 0:
  10.4 40.1 all-gather.1
  77.8 85.2 reduce-scatter.2
  261.3 29.9 reduce-scatter.4
  294.2 51.7 all-reduce.6
where the time goes:
time: 356 us; the launch traced here: 355 us
  waiting for transfers between devices  200 us (56%)
  blocking collectives  87.9 us (25%)
  matrix products  34.3 us (10%)
  between operations  17 us (5%)
  local copies, waits for them, and re-layouts  10.5 us (3%)
  other arithmetic  5.36 us (2%)
    reduce_scatter x1, waiting for transfers between devices, shards(): lax.psum_scatter(partial_proj, 'vocab', scatter_dimension=1, tiled=True)  76.5 us
    unnamed x5, waiting for transfers between devices  52.9 us
    all_gather x1, waiting for transfers between devices, shards(): piece = lax.all_gather(key_value, 'ctx', axis=1, tiled=True)  40.3 us
    psum x1, blocking collectives, shards(): lax.psum((local_total, local_target), ('ctx', 'vocab'))  38 us
    reduce_scatter x1, waiting for transfers between devices, shards(): lax.psum_scatter(partial_grad, 'vocab', scatter_dimension=1, tiled=True)  30.1 us
    all_gather x1, blocking collectives, shards(): normed_full = lax.all_gather(normed, 'vocab', axis=1, tiled=True)  13.2 us
    psum x1, blocking collectives, shards(): lax.psum(jnp.sum(own_cols * own_cols, axis=1, keepdims=True), 'vocab')  10.9 us
    all_gather x1, blocking collectives, shards(): lax.all_gather(normed_full, 'ctx', axis=0, tiled=True)  10.4 us
  transfers between devices with their start and end apart: 4, of which 4 were waited for; matrix products, arithmetic and copies ran while one was open for 0% of the time, Pallas kernels for 0%

commit v1 on v0

--- a/solution.py
+++ b/solution.py
@@ -1,6 +1,11 @@
+import functools
+import math
+
 import jax
 import jax.numpy as jnp
 from jax import lax
+from jax.experimental import pallas as pl
+from jax.experimental.pallas import tpu as pltpu
 from jax.sharding import PartitionSpec as P
 
 D = 4608
@@ -14,6 +19,7 @@
 logit_cap = 30.0
 query_scalar = 144.0
 epsilon = 1e-06
+MESH = pl.DeviceIdType.MESH
 
 
 def attend(key_value, query_grp, query_pos):
@@ -123,6 +129,488 @@
     return (final_hidden, mean_loss, grad_normed)
 
 
+def flip(index, offset):
+    moved, bit = 0, 1
+    while bit <= offset or bit == 1:
+        here = lax.rem(index // bit, 2)
+        moved = moved + bit * (lax.rem(here + (offset // bit) % 2, 2) - here)
+        bit *= 2
+    return index + moved
+
+
+def fused_kernel(
+    n, vn, q, k, v, res, w_hbm, post, final, e_hbm, tm, pos,
+    hid_out, loss_out, grad_out,
+    q_all, k_all, v_all, out_all, att, w_buf, e_buf, part, own, up, down, sq_all, pick_z, gain_z,
+    pick_all, tm_all, tot_z, tot_p, gsend, grecv, zsend, zrecv, acc,
+    w_sem, e_sem, qs, qr, ks, kr, vs, vr, fks, fkr, fvs, fvr, outs, outr, ups, upr, dns, dnr,
+    sqs, sqr, pzs, pzr, gns, gnr, pas, par, tms, tmr, tzs, tzr, tps, tpr, gs, gr, zs, zr,
+):
+    me, z = lax.axis_index("ctx"), lax.axis_index("vocab")
+    tok, feat = res.shape
+    model = vn * feat
+    half = model // 2
+    picks = tm.shape[0]
+    total_picks = n * picks
+    vocab_local = e_buf.shape[0]
+    chunks = ups.shape[1]
+    rows = tok // chunks
+    f32 = jnp.float32
+
+    def plane(i):
+        return {"ctx": i, "vocab": z}
+
+    def column(i):
+        return {"ctx": me, "vocab": i}
+
+    def copy(src, dst, send, recv, device):
+        return pltpu.make_async_remote_copy(
+            src_ref=src, dst_ref=dst, send_sem=send, recv_sem=recv,
+            device_id=device, device_id_type=MESH,
+        )
+
+    def lanes(i):
+        return pl.ds(pl.multiple_of(i * HEAD_DIM, HEAD_DIM), HEAD_DIM)
+
+    barrier = pltpu.get_barrier_semaphore()
+    for off in range(1, n):
+        pl.semaphore_signal(barrier, inc=1, device_id=plane(flip(me, off)), device_id_type=MESH)
+    for off in range(1, vn):
+        pl.semaphore_signal(
+            barrier, inc=1, device_id=column(lax.rem(z + off, vn)), device_id_type=MESH
+        )
+    w_copy = pltpu.make_async_copy(w_hbm, w_buf, w_sem)
+    w_copy.start()
+    chip = me // 2
+    sibling = flip(me, 1)
+    q_all[pl.ds(me, 1)] = q[:, lanes(me)][None]
+    k_all[pl.ds(me, 1)] = k[:, lanes(chip)][None]
+    v_all[pl.ds(me, 1)] = v[:, lanes(chip)][None]
+    pl.semaphore_wait(barrier, n + vn - 2)
+
+    kv_copies, q_copies, small = {}, {}, []
+    for off in (*range(2, n, 2), 1):
+        peer = flip(me, off)
+        kv_copies[off] = (
+            copy(k.at[:, lanes(peer // 2)], k_all.at[me], ks.at[off], kr.at[off], plane(peer)),
+            copy(v.at[:, lanes(peer // 2)], v_all.at[me], vs.at[off], vr.at[off], plane(peer)),
+        )
+        for c in kv_copies[off]:
+            c.start()
+    for off in range(1, n):
+        peer = flip(me, off)
+        c = copy(q.at[:, lanes(peer)], q_all.at[me], qs.at[off], qr.at[off], plane(peer))
+        c.start()
+        q_copies[off] = c
+    e_copy = pltpu.make_async_copy(e_hbm, e_buf, e_sem)
+    e_copy.start()
+    for off in range(1, n):
+        peer = flip(me, off)
+        c = copy(tm, tm_all.at[me], tms.at[off], tmr.at[off], plane(peer))
+        c.start()
+        small.append(c)
+    for off in range(1, vn):
+        c = copy(final, gain_z.at[z], gns.at[off], gnr.at[off], column(lax.rem(z + off, vn)))
+        c.start()
+        small.append(c)
+    tm_all[pl.ds(me, 1)] = tm[...][None]
+    gain_z[pl.ds(z, 1)] = final[...][None]
+    forwards = []
+    for off in range(2, n, 2):
+        source = flip(me, off)
+        for c in kv_copies[off]:
+            c.wait_recv()
+        pair = (
+            copy(k_all.at[source], k_all.at[source], fks.at[off], fkr.at[off], plane(sibling)),
+            copy(v_all.at[source], v_all.at[source], fvs.at[off], fvr.at[off], plane(sibling)),
+        )
+        for c in pair:
+            c.start()
+        forwards.extend(pair)
+    for c in kv_copies[1]:
+        c.wait_recv()
+    for off in range(1, n):
+        q_copies[off].wait_recv()
+    for c in forwards:
+        c.wait_recv()
+
+    row_id = lax.broadcasted_iota(jnp.int32, (tok, tok), 0)
+    col_id = lax.broadcasted_iota(jnp.int32, (tok, tok), 1)
+    causal = row_id >= col_id
+    pre = query_scalar ** (-0.5) / attn_cap
+    post_scale = attn_cap * math.log2(math.e)
+
+    def out_copy(i):
+        return copy(out_all.at[i], att.at[:, lanes(me)], outs.at[i], outr.at[me], plane(i))
+
+    for i in range(n - 1, -1, -1):
+        query = q_all[i]
+        total = jnp.zeros((tok, 1), f32)
+        values = jnp.zeros((tok, HEAD_DIM), f32)
+        for j in range(i + 1):
+            s = lax.dot_general(
+                query, k_all[j], (((1,), (1,)), ((), ())), preferred_element_type=f32
+            )
+            w = jnp.exp2(jnp.tanh(s * pre) * post_scale)
+            if j == i:
+                w = jnp.where(causal, w, 0.0)
+            total = total + jnp.sum(w, axis=1, keepdims=True)
+            values = values + jnp.dot(w.astype(jnp.bfloat16), v_all[j], preferred_element_type=f32)
+        out_all[i] = (values / total).astype(jnp.bfloat16)
+
+        @pl.when(me == i)
+        def _():
+            att[:, i * HEAD_DIM : (i + 1) * HEAD_DIM] = out_all[i]
+
+        @pl.when(me != i)
+        def _():
+            out_copy(i).start()
+
+    w_copy.wait()
+    for i in range(n):
+
+        @pl.when(me != i)
+        def _():
+            copy(
+                out_all.at[i], att.at[:, lanes(i)], outs.at[i], outr.at[i], plane(i)
+            ).wait_recv()
+
+    def up_copy(dst, r, source):
+        at = pl.ds(r * rows, rows)
+        return copy(
+            source.at[dst, at], up.at[dst, at], ups.at[dst, r], upr.at[dst, r],
+            column(jnp.minimum(z + 1, vn - 1)),
+        )
+
+    def down_copy(dst, r, source):
+        at = pl.ds(r * rows, rows)
+        return copy(
+            source.at[dst, at], down.at[dst, at], dns.at[dst, r], dnr.at[dst, r],
+            column(jnp.maximum(z - 1, 0)),
+        )
+
+    order = []
+    for t in range(vn):
+        for d in (vn - 1 - t, t):
+            if d not in order:
+                order.append(d)
+    for dst in order:
+        product = jnp.dot(
+            att[...], w_buf[:, dst * feat : (dst + 1) * feat], preferred_element_type=f32
+        )
+
+        @pl.when(z == dst)
+        def _():
+            own[...] = product
+
+        @pl.when(z != dst)
+        def _():
+            part[dst] = product.astype(jnp.bfloat16)
+
+        if dst > 0:
+
+            @pl.when(z == 0)
+            def _():
+                for r in range(chunks):
+                    up_copy(dst, r, part).start()
+
+        if dst < vn - 1:
+
+            @pl.when(z == vn - 1)
+            def _():
+                for r in range(chunks):
+                    down_copy(dst, r, part).start()
+
+    for t in range(vn):
+        d_up, d_down = vn - 1 - t, t
+        for r in range(chunks):
+            at = pl.ds(r * rows, rows)
+            if 1 < d_up:
+
+                @pl.when((z > 0) & (z < d_up))
+                def _():
+                    up_copy(d_up, r, up).wait_recv()
+                    up[d_up, at] = (up[d_up, at].astype(f32) + part[d_up, at].astype(f32)).astype(
+                        jnp.bfloat16
+                    )
+                    up_copy(d_up, r, up).start()
+
+            if d_down < vn - 2:
+
+                @pl.when((z < vn - 1) & (z > d_down))
+                def _():
+                    down_copy(d_down, r, down).wait_recv()
+                    down[d_down, at] = (
+                        down[d_down, at].astype(f32) + part[d_down, at].astype(f32)
+                    ).astype(jnp.bfloat16)
+                    down_copy(d_down, r, down).start()
+
+    for dst in range(vn):
+
+        @pl.when(z == dst)
+        def _():
+            for r in range(chunks):
+                at = pl.ds(r * rows, rows)
+                value = own[at]
+                if dst > 0:
+                    up_copy(dst, r, up).wait_recv()
+                    value = value + up[dst, at].astype(f32)
+                if dst < vn - 1:
+                    down_copy(dst, r, down).wait_recv()
+                    value = value + down[dst, at].astype(f32)
+                own[at] = value
+
+    cols = own[...]
+    squares = jnp.sum(cols * cols, axis=1, keepdims=True)
+    wide = jnp.transpose(jnp.broadcast_to(squares, (tok, 128)))
+    sq_all[pl.ds(z, 1)] = wide[:8][None]
+    sq_copies = []
+    for off in range(1, vn):
+        c = copy(
+            sq_all.at[z], sq_all.at[z], sqs.at[off], sqr.at[off], column(lax.rem(z + off, vn))
+        )
+        c.start()
+        sq_copies.append(c)
+    for c in sq_copies:
+        c.wait_recv()
+    summed = jnp.sum(sq_all[...], axis=0)[:1]
+    inv = lax.rsqrt(summed / model + epsilon)
+    inv = jnp.transpose(jnp.broadcast_to(inv, (128, tok)))[:, :1]
+    hidden = (res[...].astype(f32) + cols * inv * post[...]).astype(jnp.bfloat16)
+    hid_out[...] = hidden
+    chosen = pos[...] == lax.broadcasted_iota(jnp.int32, (picks, tok), 1)
+    picked = jnp.dot(chosen.astype(f32).astype(jnp.bfloat16), hidden, preferred_element_type=f32)
+    pick_z[pl.ds(z, 1)] = picked[None]
+    pz_copies = []
+    for off in range(1, vn):
+        c = copy(
+            pick_z.at[z], pick_z.at[z], pzs.at[off], pzr.at[off], column(lax.rem(z + off, vn))
+        )
+        c.start()
+        pz_copies.append(c)
+    for c in pz_copies:
+        c.wait_recv()
+    for c in small:
+        c.wait_recv()
+    whole = jnp.concatenate([pick_z[i] for i in range(vn)], axis=1)
+    gain = jnp.concatenate([gain_z[i] for i in range(vn)], axis=1)
+    scale = lax.rsqrt(jnp.sum(whole * whole, axis=1, keepdims=True) / model + epsilon)
+    normed = whole * scale * gain
+    pick_all[pl.ds(me, 1)] = (
+        jnp.concatenate([normed[:, :half], normed[:, half:]], axis=0).astype(jnp.bfloat16)[None]
+    )
+    pa_copies = {}
+    for off in (*range(2, n, 2), 1):
+        pa_copies[off] = copy(
+            pick_all.at[me], pick_all.at[me], pas.at[off], par.at[off], plane(flip(me, off))
+        )
+        pa_copies[off].start()
+    passed = []
+    for off in range(2, n, 2):
+        source = flip(me, off)
+        pa_copies[off].wait_recv()
+        c = copy(
+            pick_all.at[source], pick_all.at[source], pas.at[off + 1], par.at[off + 1],
+            plane(sibling),
+        )
+        c.start()
+        passed.append(c)
+    pa_copies[1].wait_recv()
+    for c in passed:
+        c.wait_recv()
+    e_copy.wait()
+    left, right = [], []
+    for i in range(n):
+        block = pick_all[i].astype(f32)
+        left.append(block[:picks])
+        right.append(block[picks:])
+    states = jnp.concatenate(
+        [jnp.concatenate(left, axis=0), jnp.concatenate(right, axis=0)], axis=1
+    ).astype(jnp.bfloat16)
+    raw = lax.dot_general(
+        states, e_buf[...], (((1,), (1,)), ((), ())), preferred_element_type=f32
+    )
+    ratio = jnp.tanh(raw / logit_cap)
+    logits = logit_cap * ratio
+    tm_rows = tm_all[...].reshape(total_picks, 128)
+    target = tm_rows[:, :1]
+    mask = tm_rows[:, 64:65].astype(f32)
+    base = (me * vn + z) * vocab_local
+    onehot = base + lax.broadcasted_iota(jnp.int32, (total_picks, vocab_local), 1) == target
+    exp_logits = jnp.exp(logits)
+    slope = 1.0 - ratio * ratio
+    local_total = jnp.sum(exp_logits, axis=1, keepdims=True)
+    local_target = jnp.sum(jnp.where(onehot, logits, 0.0), axis=1, keepdims=True)
+    target_slope = jnp.sum(jnp.where(onehot, slope, 0.0), axis=1, keepdims=True)
+    target_exp = jnp.sum(jnp.where(onehot, exp_logits, 0.0), axis=1, keepdims=True)
+    lane = lax.broadcasted_iota(jnp.int32, (total_picks, 128), 1)
+    packed = jnp.where(lane == 0, local_total, jnp.where(lane == 1, local_target, 0.0))
+    packed = jnp.concatenate([packed, jnp.zeros((128 - total_picks, 128), f32)], axis=0)
+    tot_z[pl.ds(z, 1)] = jnp.transpose(packed)[:8][None]
+    tz_copies = []
+    for off in range(1, vn):
+        c = copy(tot_z.at[z], tot_z.at[z], tzs.at[off], tzr.at[off], column(lax.rem(z + off, vn)))
+        c.start()
+        tz_copies.append(c)
+    weights = jnp.concatenate(
+        [jnp.where(onehot, 0.0, exp_logits * slope), jnp.where(onehot, 1.0, 0.0)], axis=0
+    ).astype(jnp.bfloat16)
+    for c in tz_copies:
+        c.wait_recv()
+    tot_p[pl.ds(me, 1)] = jnp.sum(tot_z[...], axis=0)[None]
+    tp_copies = []
+    for off in range(1, n):
+        c = copy(tot_p.at[me], tot_p.at[me], tps.at[off], tpr.at[off], plane(flip(me, off)))
+        c.start()
+        tp_copies.append(c)
+    acc[...] = jnp.dot(weights, e_buf[...], preferred_element_type=f32)
+    for c in tp_copies:
+        c.wait_recv()
+    sums = jnp.sum(tot_p[...], axis=0)
+    sums = jnp.transpose(jnp.concatenate([sums, jnp.zeros((120, 128), f32)], axis=0))
+    totals = sums[:total_picks, :1]
+    target_logit = sums[:total_picks, 1:2]
+    loss = jnp.sum(mask * (jnp.log(totals) - target_logit), axis=0, keepdims=True) / total_picks
+    loss_out[...] = jnp.broadcast_to(loss, loss_out.shape)
+    other = mask / totals
+    at_target = (mask * (target_exp / totals - 1.0) * target_slope).astype(jnp.bfloat16).astype(f32)
+    grad = other * acc[:total_picks] + at_target * acc[total_picks:]
+    for i in range(n):
+        block = grad[i * picks : (i + 1) * picks]
+        gsend[i] = jnp.concatenate([block[:, :half], block[:, half:]], axis=0).astype(jnp.bfloat16)
+    g_copies = []
+    for off in (*range(2, n), 1):
+        peer = flip(me, off)
+        c = copy(gsend.at[peer], grecv.at[me], gs.at[off], gr.at[off], plane(peer))
+        c.start()
+        g_copies.append(c)
+    grecv[pl.ds(me, 1)] = gsend[pl.ds(me, 1)]
+    for c in g_copies:
+        c.wait_recv()
+    both = grecv[0].astype(f32)
+    for i in range(1, n):
+        both = both + grecv[i].astype(f32)
+    mine = jnp.concatenate([both[:picks], both[picks:]], axis=1)
+    for i in range(vn):
+        zsend[i] = mine[:, i * feat : (i + 1) * feat]
+    z_copies = []
+    for off in range(1, vn):
+        peer = lax.rem(z + off, vn)
+        c = copy(zsend.at[peer], zrecv.at[z], zs.at[off], zr.at[off], column(peer))
+        c.start()
+        z_copies.append(c)
+    zrecv[pl.ds(z, 1)] = zsend[pl.ds(z, 1)]
+    for c in z_copies:
+        c.wait_recv()
+    grad_out[...] = jnp.sum(zrecv[...], axis=0)
+
+    for pair in kv_copies.values():
+        for c in pair:
+            c.wait_send()
+    for group in (
+        q_copies.values(), small, forwards, sq_copies, pz_copies, pa_copies.values(), passed,
+        tz_copies, tp_copies, g_copies, z_copies,
+    ):
+        for c in group:
+            c.wait_send()
+    for i in range(n):
+
+        @pl.when(me != i)
+        def _():
+            out_copy(i).wait_send()
+
+    for dst in range(vn):
+        for r in range(chunks):
+
+            @pl.when(z < dst)
+            def _():
+                up_copy(dst, r, up).wait_send()
+
+            @pl.when(z > dst)
+            def _():
+                down_copy(dst, r, down).wait_send()
+
+
+def fused(
+    n, vn, query_rows, key_rows, value_rows, residual, out_weight, post_gain, final_gain,
+    embedding, targets, loss_mask, pick_pos,
+):
+    tok, feat = residual.shape
+    model = vn * feat
+    picks = targets.shape[0]
+    bf16, f32, i32 = jnp.bfloat16, jnp.float32, jnp.int32
+    chunks = 4
+    first = jnp.broadcast_to(targets[:, None], (picks, 64))
+    second = jnp.broadcast_to(loss_mask[:, None], (picks, 64))
+    tm = jnp.concatenate([first, second], axis=1)
+    dma = pltpu.SemaphoreType.DMA
+    vmem = pl.BlockSpec(memory_space=pltpu.VMEM)
+    hbm = pl.BlockSpec(memory_space=pl.ANY)
+    sems = [dma, dma] + [dma((n,))] * 12 + [dma((vn, chunks))] * 4 + [dma((vn,))] * 6
+    sems += [dma((n,))] * 4 + [dma((vn,))] * 2 + [dma((n,))] * 4 + [dma((vn,))] * 2
+    hidden, loss, grad = pl.pallas_call(
+        functools.partial(fused_kernel, n, vn),
+        out_shape=(
+            jax.ShapeDtypeStruct((tok, feat), bf16),
+            jax.ShapeDtypeStruct((8, 128), f32),
+            jax.ShapeDtypeStruct((picks, feat), f32),
+        ),
+        in_specs=[vmem, vmem, vmem, vmem, hbm, vmem, vmem, hbm, vmem, vmem],
+        out_specs=(vmem, vmem, vmem),
+        scratch_shapes=[
+            pltpu.VMEM((n, tok, HEAD_DIM), bf16),
+            pltpu.VMEM((n, tok, HEAD_DIM), bf16),
+            pltpu.VMEM((n, tok, HEAD_DIM), bf16),
+            pltpu.VMEM((n, tok, HEAD_DIM), bf16),
+            pltpu.VMEM((tok, n * HEAD_DIM), bf16),
+            pltpu.VMEM(out_weight.shape, bf16),
+            pltpu.VMEM(embedding.shape, bf16),
+            pltpu.VMEM((vn, tok, feat), bf16),
+            pltpu.VMEM((tok, feat), f32),
+            pltpu.VMEM((vn, tok, feat), bf16),
+            pltpu.VMEM((vn, tok, feat), bf16),
+            pltpu.VMEM((vn, 8, tok), f32),
+            pltpu.VMEM((vn, picks, feat), f32),
+            pltpu.VMEM((vn, picks, feat), f32),
+            pltpu.VMEM((n, 2 * picks, model // 2), bf16),
+            pltpu.VMEM((n, picks, 128), i32),
+            pltpu.VMEM((vn, 8, 128), f32),
+            pltpu.VMEM((n, 8, 128), f32),
+            pltpu.VMEM((n, 2 * picks, model // 2), bf16),
+            pltpu.VMEM((n, 2 * picks, model // 2), bf16),
+            pltpu.VMEM((vn, picks, feat), f32),
+            pltpu.VMEM((vn, picks, feat), f32),
+            pltpu.VMEM((2 * n * picks, model), f32),
+            *sems,
+        ],
+        compiler_params=pltpu.CompilerParams(
+            collective_id=0, has_side_effects=True, vmem_limit_bytes=60 * 1024 * 1024
+        ),
+    )(
+        query_rows, key_rows, value_rows, residual, out_weight, post_gain[None, :],
+        jnp.broadcast_to(final_gain[None, :], (picks, feat)), embedding, tm, pick_pos[:, None],
+    )
+    return hidden, loss[0, 0], grad
+
+
+def fits(n, vn, query_rows, key_rows, residual, targets):
+    heads, kv = query_rows.shape[1] // HEAD_DIM, key_rows.shape[1] // HEAD_DIM
+    tok, feat = residual.shape
+    return (
+        n >= 2
+        and n & (n - 1) == 0
+        and heads == n
+        and heads == 2 * kv
+        and vn >= 2
+        and n * tok <= WINDOW
+        and tok % 128 == 0
+        and feat % 128 == 0
+        and (vn * feat) % 256 == 0
+        and targets.shape[0] == 8
+        and n * targets.shape[0] <= 128
+    )
+
+
 def solution(mesh):
     in_specs = (
         P("ctx", "vocab"),
@@ -138,4 +626,11 @@
         P("ctx"),
     )
     out_specs = (P("ctx", "vocab"), P(), P("ctx", "vocab"))
-    return jax.shard_map(shards, mesh=mesh, in_specs=in_specs, out_specs=out_specs, check_vma=False)
+    n, vn = mesh.shape["ctx"], mesh.shape["vocab"]
+
+    def local(*args):
+        if fits(n, vn, args[0], args[1], args[3], args[8]):
+            return fused(n, vn, *args)
+        return shards(*args)
+
+    return jax.shard_map(local, mesh=mesh, in_specs=in_specs, out_specs=out_specs, check_vma=False)

time: 356 us -> 139 us (0.39)
  waiting for transfers between devices: 200 us -> 0 us
  Pallas kernels: 0 us -> 127 us
  blocking collectives: 87.9 us -> 0 us
  matrix products: 34.3 us -> 0 us
  between operations: 17 us -> 0.64 us
  other arithmetic: 5.36 us -> 0.65 us
    pallas_call x0 -> x1, Pallas kernels: none -> 127 us  [fused(): pl.pallas_call(functools.partial(fused_kernel, n, vn), out_shape=(jax.Sha...]
    reduce_scatter x2 -> x0, waiting for transfers between devices: 107 us -> none  [the longest x1 76.5 us: shards(): lax.psum_scatter(partial_proj, 'vocab', scatter_dimension=1, tiled=True)]
    psum x3 -> x0, blocking collectives: 57.3 us -> none  [the longest x1 38 us: shards(): lax.psum((local_total, local_target), ('ctx', 'vocab'))]
    unnamed x5 -> x0, waiting for transfers between devices: 52.9 us -> none
    all_gather x1 -> x0, waiting for transfers between devices: 40.3 us -> none  [shards(): piece = lax.all_gather(key_value, 'ctx', axis=1, tiled=True)]
    dot_general x4 -> x0, matrix products: 28.2 us -> none  [the longest x1 8.02 us: shards(): jnp.dot(attended, out_weight, preferred_element_type=jnp.float32)]
    all_gather x2 -> x0, blocking collectives: 23.5 us -> none  [the longest x1 13.2 us: shards(): normed_full = lax.all_gather(normed, 'vocab', axis=1, tiled=True)]
    unnamed x1 -> x0, blocking collectives: 7.02 us -> none
  transfers between devices with their start and end apart: 4 -> 0, of which waited for: 4 -> 0; matrix products, arithmetic and copies ran while one was open for 0% -> 0% of each run, Pallas kernels for 0% -> 0%
where the time goes in v1:
time: 139 us; the launch traced here: 138 us
  Pallas kernels  127 us (91%)
  local copies, waits for them, and re-layouts  9.87 us (7%)
    pallas_call x1, Pallas kernels, fused(): pl.pallas_call(functools.partial(fused_kernel, n, vn), out_shape=(jax.Sha...  127 us
    unnamed x2, local copies, waits for them, and re-layouts  3.31 us

profile of v1, /device:TPU:0, one launch (start us, length us, event | category | flops | bytes accessed | tf_op | source)
XLA Modules:
  0.0 138.3 jit_solution(17877414512298372269)
XLA Ops:
  0.6 0.7 broadcast_in_dim.12
  1.4 0.7 broadcast_in_dim.13
  2.1 0.7 pad_add_fusion.tm
  2.7 1.3 copy.14.pos
  4.1 1.3 broadcast_in_dim.10.post
  5.3 1.3 broadcast_in_dim.11.final
  6.7 127.1 %shard_map.130 = (bf16[256,1152]{1,0:T(8,128)(2,1)}, f32[8,128]{1,0:T(8,128)}, f32[8,1152]{1,0:T(8,128)}) custom-call(bf16[256,1024]{1,0:T(8,128)(2,1)} %q.1, bf16[256,512]{1,0:T(8,128)(2,1)} %k.1, bf16[256,512]{1,0:T(8,128)(2,1)} %v.1, bf16[256,1152]{1,0:T(8,128)(2,1)} %res.1, bf16[1024,4608]{1,0:T(8,128)(2,1)} %w_hbm.1, f32[1,1152]{1,0:T(1,128)} %broadcast_in_dim.10.post, ...), custom_call_target="tpu_custom_call" | custom-call | tf_op jit(solution)/shard_map/pallas_call | solution.py:551
  133.8 1.2 slice.3
  135.0 1.9 %copy.17 = bf16[256,1152]{1,0:T(8,128)(2,1)} copy(bf16[256,1152]{1,0:T(8,128)(2,1)} %get-tuple-element.12) | data formatting | bytes 1179648
  136.9 1.4 %copy.18 = f32[8,1152]{1,0:T(8,128)} copy(f32[8,1152]{1,0:T(8,128)} %get-tuple-element.14) | data formatting | bytes 73728

commit v2 on v1

--- a/solution.py
+++ b/solution.py
@@ -139,12 +139,12 @@
 
 
 def fused_kernel(
-    n, vn, q, k, v, res, w_hbm, post, final, e_hbm, tm, pos,
+    n, vn, q, k, v, res, w_hbm, post, gains, e_hbm, tm, pos,
     hid_out, loss_out, grad_out,
-    q_all, k_all, v_all, out_all, att, w_buf, e_buf, part, own, up, down, sq_all, pick_z, gain_z,
+    q_all, k_all, v_all, out_all, att, w_buf, e_buf, part, own, up, down, sq_all, pick_z, gain_z, res_z, pk_send, pk_recv,
     pick_all, tm_all, tot_z, tot_p, gsend, grecv, zsend, zrecv, acc,
     w_sem, e_sem, qs, qr, ks, kr, vs, vr, fks, fkr, fvs, fvr, outs, outr, ups, upr, dns, dnr,
-    sqs, sqr, pzs, pzr, gns, gnr, pas, par, tms, tmr, tzs, tzr, tps, tpr, gs, gr, zs, zr,
+    sqs, sqr, pzs, pzr, gns, gnr, pas, par, tms, tmr, tzs, tzr, tps, tpr, gs, gr, zs, zr, rzs, rzr, pks, pkr,
 ):
     me, z = lax.axis_index("ctx"), lax.axis_index("vocab")
     tok, feat = res.shape
@@ -210,11 +210,20 @@
         c.start()
         small.append(c)
     for off in range(1, vn):
-        c = copy(final, gain_z.at[z], gns.at[off], gnr.at[off], column(lax.rem(z + off, vn)))
+        c = copy(gains, gain_z.at[z], gns.at[off], gnr.at[off], column(lax.rem(z + off, vn)))
         c.start()
         small.append(c)
     tm_all[pl.ds(me, 1)] = tm[...][None]
-    gain_z[pl.ds(z, 1)] = final[...][None]
+    gain_z[pl.ds(z, 1)] = gains[...][None]
+    chosen = pos[...] == lax.broadcasted_iota(jnp.int32, (picks, tok), 1)
+    chosen = chosen.astype(f32).astype(jnp.bfloat16)
+    res_z[pl.ds(z, 1)] = jnp.dot(chosen, res[...], preferred_element_type=f32)[None]
+    for off in range(1, vn):
+        c = copy(
+            res_z.at[z], res_z.at[z], rzs.at[off], rzr.at[off], column(lax.rem(z + off, vn))
+        )
+        c.start()
+        small.append(c)
     forwards = []
     for off in range(2, n, 2):
         source = flip(me, off)
@@ -294,6 +303,54 @@
         for d in (vn - 1 - t, t):
             if d not in order:
                 order.append(d)
+    att_pick = jnp.dot(chosen, att[...], preferred_element_type=f32).astype(jnp.bfloat16)
+    for dst in order:
+        pk_send[dst] = jnp.dot(
+            att_pick, w_buf[:, dst * feat : (dst + 1) * feat], preferred_element_type=f32
+        )
+    pk_copies = []
+    for off in range(1, vn):
+        peer = lax.rem(z + off, vn)
+        c = copy(pk_send.at[peer], pk_recv.at[z], pks.at[off], pkr.at[off], column(peer))
+        c.start()
+        pk_copies.append(c)
+    pk_recv[pl.ds(z, 1)] = pk_send[pl.ds(z, 1)]
+    count = (vn - 1) * chunks
+    shares = (1, 2, 5, 6, 9, 12)
+
+    def sent(point):
+        if point < 0:
+            return 0
+        if point >= len(shares):
+            return count
+        return count * shares[point] // shares[-1]
+
+    def move(level, index):
+        t, r = index // chunks, index % chunks
+        at = pl.ds(r * rows, rows)
+        if t >= vn - 1 - level:
+            return
+        for here, dst, buffer, link in (
+            (level, vn - 1 - t, up, up_copy),
+            (vn - 1 - level, t, down, down_copy),
+        ):
+
+            @pl.when(z == here)
+            def _():
+                if level == 0:
+                    link(dst, r, part).start()
+                else:
+                    link(dst, r, buffer).wait_recv()
+                    buffer[dst, at] = (
+                        buffer[dst, at].astype(f32) + part[dst, at].astype(f32)
+                    ).astype(jnp.bfloat16)
+                    link(dst, r, buffer).start()
+
+    def advance(point):
+        for level in range(vn - 1):
+            for index in range(sent(point - level - 1), sent(point - level)):
+                move(level, index)
+
     for dst in order:
         product = jnp.dot(
             att[...], w_buf[:, dst * feat : (dst + 1) * feat], preferred_element_type=f32
@@ -307,80 +364,10 @@
         def _():
             part[dst] = product.astype(jnp.bfloat16)
 
-        if dst > 0:
-
-            @pl.when(z == 0)
-            def _():
-                for r in range(chunks):
-                    up_copy(dst, r, part).start()
-
-        if dst < vn - 1:
-
-            @pl.when(z == vn - 1)
-            def _():
-                for r in range(chunks):
-                    down_copy(dst, r, part).start()
-
-    for t in range(vn):
-        d_up, d_down = vn - 1 - t, t
-        for r in range(chunks):
-            at = pl.ds(r * rows, rows)
-            if 1 < d_up:
-
-                @pl.when((z > 0) & (z < d_up))
-                def _():
-                    up_copy(d_up, r, up).wait_recv()
-                    up[d_up, at] = (up[d_up, at].astype(f32) + part[d_up, at].astype(f32)).astype(
-                        jnp.bfloat16
-                    )
-                    up_copy(d_up, r, up).start()
-
-            if d_down < vn - 2:
-
-                @pl.when((z < vn - 1) & (z > d_down))
-                def _():
-                    down_copy(d_down, r, down).wait_recv()
-                    down[d_down, at] = (
-                        down[d_down, at].astype(f32) + part[d_down, at].astype(f32)
-                    ).astype(jnp.bfloat16)
-                    down_copy(d_down, r, down).start()
-
-    for dst in range(vn):
-
-        @pl.when(z == dst)
-        def _():
-            for r in range(chunks):
-                at = pl.ds(r * rows, rows)
-                value = own[at]
-                if dst > 0:
-                    up_copy(dst, r, up).wait_recv()
-                    value = value + up[dst, at].astype(f32)
-                if dst < vn - 1:
-                    down_copy(dst, r, down).wait_recv()
-                    value = value + down[dst, at].astype(f32)
-                own[at] = value
-
-    cols = own[...]
-    squares = jnp.sum(cols * cols, axis=1, keepdims=True)
-    wide = jnp.transpose(jnp.broadcast_to(squares, (tok, 128)))
-    sq_all[pl.ds(z, 1)] = wide[:8][None]
-    sq_copies = []
-    for off in range(1, vn):
-        c = copy(
-            sq_all.at[z], sq_all.at[z], sqs.at[off], sqr.at[off], column(lax.rem(z + off, vn))
-        )
-        c.start()
-        sq_copies.append(c)
-    for c in sq_copies:
-        c.wait_recv()
-    summed = jnp.sum(sq_all[...], axis=0)[:1]
-    inv = lax.rsqrt(summed / model + epsilon)
-    inv = jnp.transpose(jnp.broadcast_to(inv, (128, tok)))[:, :1]
-    hidden = (res[...].astype(f32) + cols * inv * post[...]).astype(jnp.bfloat16)
-    hid_out[...] = hidden
-    chosen = pos[...] == lax.broadcasted_iota(jnp.int32, (picks, tok), 1)
-    picked = jnp.dot(chosen.astype(f32).astype(jnp.bfloat16), hidden, preferred_element_type=f32)
-    pick_z[pl.ds(z, 1)] = picked[None]
+    advance(0)
+    for c in pk_copies:
+        c.wait_recv()
+    pick_z[pl.ds(z, 1)] = jnp.sum(pk_recv[...], axis=0)[None]
     pz_copies = []
     for off in range(1, vn):
         c = copy(
@@ -388,12 +375,17 @@
         )
         c.start()
         pz_copies.append(c)
+    advance(1)
+    for c in small:
+        c.wait_recv()
     for c in pz_copies:
         c.wait_recv()
-    for c in small:
-        c.wait_recv()
-    whole = jnp.concatenate([pick_z[i] for i in range(vn)], axis=1)
-    gain = jnp.concatenate([gain_z[i] for i in range(vn)], axis=1)
+    proj = jnp.concatenate([pick_z[i] for i in range(vn)], axis=1)
+    gain = jnp.concatenate([gain_z[i, :picks] for i in range(vn)], axis=1)
+    gain_post = jnp.concatenate([gain_z[i, picks:] for i in range(vn)], axis=1)
+    res_pick = jnp.concatenate([res_z[i] for i in range(vn)], axis=1)
+    scale = lax.rsqrt(jnp.sum(proj * proj, axis=1, keepdims=True) / model + epsilon)
+    whole = (res_pick + proj * scale * gain_post).astype(jnp.bfloat16).astype(f32)
     scale = lax.rsqrt(jnp.sum(whole * whole, axis=1, keepdims=True) / model + epsilon)
     normed = whole * scale * gain
     pick_all[pl.ds(me, 1)] = (
@@ -405,6 +397,7 @@
             pick_all.at[me], pick_all.at[me], pas.at[off], par.at[off], plane(flip(me, off))
         )
         pa_copies[off].start()
+    advance(2)
     passed = []
     for off in range(2, n, 2):
         source = flip(me, off)
@@ -452,6 +445,7 @@
         c = copy(tot_z.at[z], tot_z.at[z], tzs.at[off], tzr.at[off], column(lax.rem(z + off, vn)))
         c.start()
         tz_copies.append(c)
+    advance(3)
     weights = jnp.concatenate(
         [jnp.where(onehot, 0.0, exp_logits * slope), jnp.where(onehot, 1.0, 0.0)], axis=0
     ).astype(jnp.bfloat16)
@@ -485,6 +479,7 @@
         c.start()
         g_copies.append(c)
     grecv[pl.ds(me, 1)] = gsend[pl.ds(me, 1)]
+    advance(4)
     for c in g_copies:
         c.wait_recv()
     both = grecv[0].astype(f32)
@@ -500,6 +495,41 @@
         c.start()
         z_copies.append(c)
     zrecv[pl.ds(z, 1)] = zsend[pl.ds(z, 1)]
+    for point in range(5, len(shares) + vn - 1):
+        advance(point)
+    for dst in range(vn):
+
+        @pl.when(z == dst)
+        def _():
+            for r in range(chunks):
+                at = pl.ds(r * rows, rows)
+                value = own[at]
+                if dst > 0:
+                    up_copy(dst, r, up).wait_recv()
+                    value = value + up[dst, at].astype(f32)
+                if dst < vn - 1:
+                    down_copy(dst, r, down).wait_recv()
+                    value = value + down[dst, at].astype(f32)
+                own[at] = value
+
+    cols = own[...]
+    squares = jnp.sum(cols * cols, axis=1, keepdims=True)
+    wide = jnp.transpose(jnp.broadcast_to(squares, (tok, 128)))
+    sq_all[pl.ds(z, 1)] = wide[:8][None]
+    sq_copies = []
+    for off in range(1, vn):
+        c = copy(
+            sq_all.at[z], sq_all.at[z], sqs.at[off], sqr.at[off], column(lax.rem(z + off, vn))
+        )
+        c.start()
+        sq_copies.append(c)
+    for c in sq_copies:
+        c.wait_recv()
+    summed = jnp.sum(sq_all[...], axis=0)[:1]
+    inv = lax.rsqrt(summed / model + epsilon)
+    inv = jnp.transpose(jnp.broadcast_to(inv, (128, tok)))[:, :1]
+    hidden = (res[...].astype(f32) + cols * inv * post[...]).astype(jnp.bfloat16)
+    hid_out[...] = hidden
     for c in z_copies:
         c.wait_recv()
     grad_out[...] = jnp.sum(zrecv[...], axis=0)
@@ -508,7 +538,7 @@
         for c in pair:
             c.wait_send()
     for group in (
-        q_copies.values(), small, forwards, sq_copies, pz_copies, pa_copies.values(), passed,
+        q_copies.values(), small, forwards, sq_copies, pk_copies, pz_copies, pa_copies.values(), passed,
         tz_copies, tp_copies, g_copies, z_copies,
     ):
         for c in group:
@@ -543,11 +573,14 @@
     first = jnp.broadcast_to(targets[:, None], (picks, 64))
     second = jnp.broadcast_to(loss_mask[:, None], (picks, 64))
     tm = jnp.concatenate([first, second], axis=1)
+    gains = jnp.concatenate(
+        [jnp.broadcast_to(g[None, :], (picks, feat)) for g in (final_gain, post_gain)], axis=0
+    )
     dma = pltpu.SemaphoreType.DMA
     vmem = pl.BlockSpec(memory_space=pltpu.VMEM)
     hbm = pl.BlockSpec(memory_space=pl.ANY)
     sems = [dma, dma] + [dma((n,))] * 12 + [dma((vn, chunks))] * 4 + [dma((vn,))] * 6
-    sems += [dma((n,))] * 4 + [dma((vn,))] * 2 + [dma((n,))] * 4 + [dma((vn,))] * 2
+    sems += [dma((n,))] * 4 + [dma((vn,))] * 2 + [dma((n,))] * 4 + [dma((vn,))] * 6
     hidden, loss, grad = pl.pallas_call(
         functools.partial(fused_kernel, n, vn),
         out_shape=(
@@ -571,6 +604,9 @@
             pltpu.VMEM((vn, tok, feat), bf16),
             pltpu.VMEM((vn, 8, tok), f32),
             pltpu.VMEM((vn, picks, feat), f32),
+            pltpu.VMEM((vn, 2 * picks, feat), f32),
+            pltpu.VMEM((vn, picks, feat), f32),
+            pltpu.VMEM((vn, picks, feat), f32),
             pltpu.VMEM((vn, picks, feat), f32),
             pltpu.VMEM((n, 2 * picks, model // 2), bf16),
             pltpu.VMEM((n, picks, 128), i32),
@@ -588,7 +624,7 @@
         ),
     )(
         query_rows, key_rows, value_rows, residual, out_weight, post_gain[None, :],
-        jnp.broadcast_to(final_gain[None, :], (picks, feat)), embedding, tm, pick_pos[:, None],
+        gains, embedding, tm, pick_pos[:, None],
     )
     return hidden, loss[0, 0], grad
 

time: 139 us -> 106 us (0.76)
  Pallas kernels: 127 us -> 93.2 us
    pallas_call x1, Pallas kernels: 127 us -> 93.2 us  [fused(): pl.pallas_call(functools.partial(fused_kernel, n, vn), out_shape=(jax.Sha...]
where the time goes in v2:
time: 106 us; the launch traced here: 105 us
  Pallas kernels  93.2 us (88%)
  local copies, waits for them, and re-layouts  9.95 us (9%)
  other arithmetic  1.29 us (1%)
    pallas_call x1, Pallas kernels, fused(): pl.pallas_call(functools.partial(fused_kernel, n, vn), out_shape=(jax.Sha...  93.2 us
    unnamed x2, local copies, waits for them, and re-layouts  3.31 us

profile of v2, /device:TPU:0, one launch (start us, length us, event | category | flops | bytes accessed | tf_op | source)
XLA Modules:
  0.0 105.1 jit_solution(3454514331160039330)
XLA Ops:
  0.6 0.7 broadcast_in_dim.15
  1.4 0.7 broadcast_in_dim.16
  2.1 0.7 pad_add_fusion.tm
  2.7 1.3 %copy.14.pos = s32[8,1]{1,0:T(8,128)} copy(s32[8,1]{0,1:T(1,128)} %bitcast.2) | data formatting | bytes 64 | tf_op jit(solution)/shard_map/broadcast_in_dim | solution.py:627
  4.1 1.3 %broadcast_in_dim.12.post = f32[1,1152]{1,0:T(1,128)} reshape(f32[1152]{0:T(1024)} %param.16) | data formatting | bytes 9216 | tf_op jit(solution)/shard_map/broadcast_in_dim | solution.py:626
  5.3 0.7 broadcast_in_dim.13
  6.0 0.7 broadcast_in_dim.14
  6.7 0.6 pad_maximum_fusion.gains
  7.4 93.2 %shard_map.130 = (bf16[256,1152]{1,0:T(8,128)(2,1)}, f32[8,128]{1,0:T(8,128)}, f32[8,1152]{1,0:T(8,128)}) custom-call(bf16[256,1024]{1,0:T(8,128)(2,1)} %q.1, bf16[256,512]{1,0:T(8,128)(2,1)} %k.1, bf16[256,512]{1,0:T(8,128)(2,1)} %v.1, bf16[256,1152]{1,0:T(8,128)(2,1)} %res.1, bf16[1024,4608]{1,0:T(8,128)(2,1)} %w_hbm.1, f32[1,1152]{1,0:T(1,128)} %broadcast_in_dim.12.post, ...), custom_call_target="tpu_custom_call" | custom-call | tf_op jit(solution)/shard_map/pallas_call | solution.py:584
  100.6 1.2 %slice.3 = f32[1,1]{1,0:T(1,128)} slice(f32[8,128]{1,0:T(8,128)} %get-tuple-element.7), slice={[0:1], [0:1]} | slice | bytes 8 | tf_op jit(solution)/shard_map/slice | solution.py:629
  101.8 1.9 %copy.17 = bf16[256,1152]{1,0:T(8,128)(2,1)} copy(bf16[256,1152]{1,0:T(8,128)(2,1)} %get-tuple-element.12) | data formatting | bytes 1179648
  103.7 1.4 %copy.18 = f32[8,1152]{1,0:T(8,128)} copy(f32[8,1152]{1,0:T(8,128)} %get-tuple-element.14) | data formatting | bytes 73728
